TPU v7x, 32 devices: a whole 2x2x4 slice. The times are simulated.
32 devices in a mesh: ctx: 8 (over z, y), head: 4 (over x, core).
Axes of the slice: x: 2, y: 2, z: 4, core: 2. Of those that a mesh axis runs over, the one named last changes fastest.
Arguments:
- queries: bfloat16 [1024, 4096], P(('ctx', 'head')), may hold values from -8 to 8
- key_rows: bfloat16 [1024, 512], P(('ctx', 'head')), may hold values from -8 to 8
- value_matrix: bfloat16 [1024, 512], P(('ctx', 'head')), may hold values from -6 to 6
- output_gradient: bfloat16 [1024, 4096], P(('ctx', 'head')), may hold values from -6 to 6
- doc_lengths: int32 [4], replicated, may hold values from 1 to 384, as said below
Outputs:
- attended: bfloat16 [1024, 4096], P(('ctx', 'head'))
- log_norm: float32 [32, 1024], P('head', 'ctx')
- grad_queries: bfloat16 [1024, 4096], P(('ctx', 'head'))
- grad_keys: bfloat16 [1024, 512], P(('ctx', 'head'))
- grad_values: bfloat16 [1024, 512], P(('ctx', 'head'))
Inputs may be any that keep to these rules, and one draw needn't show every extreme that they name: `doc_lengths`: 4 document lengths in order; they sum to 1024, and the longest is exactly 384.
All inputs are finite; a program needn't handle non-finite values.
Results may differ from a plain program's by a relative error of at most 0.017.
Values may be sent and summed in bfloat16 or wider, within the bound.
A program may use at most 64 MiB of HBM per device.

v0:
```python
import math

import jax
import jax.numpy as jnp
from jax import lax
from jax.sharding import PartitionSpec as P

HEAD_WIDTH = 128


neg_fill = -1e30


def passed_along(value, axis, by):
    count = lax.axis_size(axis)
    pairs = [(i, i + by) for i in range(count) if 0 <= i + by < count]
    return lax.ppermute(value, axis, pairs)


def doc_numbers(positions, doc_lengths):
    bounds = jnp.cumsum(doc_lengths)
    counted = jnp.sum((positions[:, None] >= bounds[None, :]).astype(jnp.int32), axis=1)
    return jnp.where(positions >= 0, counted, -1)


def attend(query_rows, grad_rows, query_pos, window, window_pos, doc_lengths):
    tok_rows = query_rows.shape[0]
    kv_cols = window.shape[1] // 2
    kv_heads = kv_cols // HEAD_WIDTH
    group_width = query_rows.shape[1] // kv_cols
    score_scale = 1.0 / math.sqrt(HEAD_WIDTH)
    window_len = window.shape[0]
    query_doc = doc_numbers(query_pos, doc_lengths)
    window_doc = doc_numbers(window_pos, doc_lengths)
    key_block_len = min(512, window_len)
    block_count = window_len // key_block_len
    query_heads = query_rows.reshape(tok_rows, kv_heads, group_width, HEAD_WIDTH)
    grad_heads = grad_rows.reshape(tok_rows, kv_heads, group_width, HEAD_WIDTH)

    def block_scores(leading_row):
        kv_block = lax.dynamic_slice_in_dim(window, leading_row, key_block_len, 0)
        block_of_keys = kv_block[:, :kv_cols].reshape(key_block_len, kv_heads, HEAD_WIDTH)
        block_of_values = kv_block[:, kv_cols:].reshape(key_block_len, kv_heads, HEAD_WIDTH)
        scores = (
            jnp.einsum(
                "pgjd,kgd->gjpk", query_heads, block_of_keys, preferred_element_type=jnp.float32
            )
            * score_scale
        )
        block_doc = lax.dynamic_slice_in_dim(window_doc, leading_row, key_block_len, 0)
        block_pos = lax.dynamic_slice_in_dim(window_pos, leading_row, key_block_len, 0)
        visible = (query_doc[:, None] == block_doc[None, :]) & (
            block_pos[None, :] <= query_pos[:, None]
        )
        return (scores, visible, block_of_keys, block_of_values)

    def stats_step(block_idx, stats_in):
        leading_row = block_idx * key_block_len
        row_max, row_sum = stats_in
        scores, visible, block_of_keys, block_of_values = block_scores(leading_row)
        new_max = jnp.maximum(row_max, jnp.max(jnp.where(visible, scores, neg_fill), axis=3))
        weights = jnp.where(visible, jnp.exp(scores - new_max[..., None]), 0.0)
        return (new_max, row_sum * jnp.exp(row_max - new_max) + jnp.sum(weights, axis=3))

    start_max = jnp.full((kv_heads, group_width, tok_rows), neg_fill, jnp.float32)
    start_sum = jnp.zeros((kv_heads, group_width, tok_rows), jnp.float32)
    row_max, row_sum = lax.fori_loop(0, block_count, stats_step, (start_max, start_sum))
    log_total = row_max + jnp.log(row_sum)

    def output_step(block_idx, output_in):
        leading_row = block_idx * key_block_len
        scores, visible, block_of_keys, block_of_values = block_scores(leading_row)
        probabilities = jnp.where(visible, jnp.exp(scores - log_total[..., None]), 0.0).astype(
            jnp.bfloat16
        )
        return output_in + jnp.einsum(
            "gjpk,kgd->pgjd", probabilities, block_of_values, preferred_element_type=jnp.float32
        )

    attended_heads = lax.fori_loop(
        0,
        block_count,
        output_step,
        jnp.zeros((tok_rows, kv_heads, group_width, HEAD_WIDTH), jnp.float32),
    ).astype(jnp.bfloat16)
    row_delta = jnp.einsum(
        "pgjd,pgjd->gjp", grad_heads, attended_heads, preferred_element_type=jnp.float32
    )

    def grad_step(block_idx, grads_in):
        leading_row = block_idx * key_block_len
        query_acc, grad_window = grads_in
        scores, visible, block_of_keys, block_of_values = block_scores(leading_row)
        probabilities = jnp.where(visible, jnp.exp(scores - log_total[..., None]), 0.0).astype(
            jnp.bfloat16
        )
        grad_probs = jnp.einsum(
            "pgjd,kgd->gjpk", grad_heads, block_of_values, preferred_element_type=jnp.float32
        )
        score_gradient = (
            probabilities.astype(jnp.float32) * (grad_probs - row_delta[..., None]) * score_scale
        ).astype(jnp.bfloat16)
        query_acc = query_acc + jnp.einsum(
            "gjpk,kgd->pgjd", score_gradient, block_of_keys, preferred_element_type=jnp.float32
        )
        key_summands = jnp.einsum(
            "urzm,zura->mua", score_gradient, query_heads, preferred_element_type=jnp.float32
        ).reshape(key_block_len, kv_cols)
        value_summands = jnp.einsum(
            "urzm,zura->mua", probabilities, grad_heads, preferred_element_type=jnp.float32
        ).reshape(key_block_len, kv_cols)
        grad_window = lax.dynamic_update_slice_in_dim(
            grad_window, jnp.concatenate([key_summands, value_summands], axis=1), leading_row, 0
        )
        return (query_acc, grad_window)

    start_query = jnp.zeros((tok_rows, kv_heads, group_width, HEAD_WIDTH), jnp.float32)
    start_window = jnp.zeros((window_len, 2 * kv_cols), jnp.float32)
    query_acc, grad_window = lax.fori_loop(0, block_count, grad_step, (start_query, start_window))
    return (attended_heads, log_total, query_acc, grad_window)


def on_device(queries, key_rows, value_matrix, output_gradient, doc_lengths):
    queries, key_rows, value_matrix, output_gradient = (
        lax.all_to_all(queries, "head", split_axis=1, concat_axis=0, tiled=True),
        lax.all_to_all(key_rows, "head", split_axis=1, concat_axis=0, tiled=True),
        lax.all_to_all(value_matrix, "head", split_axis=1, concat_axis=0, tiled=True),
        lax.all_to_all(output_gradient, "head", split_axis=1, concat_axis=0, tiled=True),
    )
    tok_rows = queries.shape[0]
    kv_cols = key_rows.shape[1]
    kv_heads = kv_cols // HEAD_WIDTH
    group_width = queries.shape[1] // kv_cols
    ctx_count = lax.axis_size("ctx")
    reach = min(16, ctx_count // 2)
    my_index = lax.axis_index("ctx")
    query_pos = my_index * tok_rows + jnp.arange(tok_rows, dtype=jnp.int32)
    window_pos = (my_index - reach + 1) * tok_rows + jnp.arange(reach * tok_rows, dtype=jnp.int32)
    kv_pair = jnp.concatenate([key_rows, value_matrix], axis=1)
    window = kv_pair
    held_blocks = 1
    for section_idx in range(reach.bit_length()):
        if held_blocks < reach:
            need_blocks = min(held_blocks, reach - held_blocks)
            sending = window
            window = jnp.concatenate([passed_along(sending, "ctx", held_blocks), window], axis=0)
            held_blocks = held_blocks + need_blocks
    attended_heads, log_total, query_acc, grad_window = attend(
        queries, output_gradient, query_pos, window, window_pos, doc_lengths
    )
    query_bf = query_acc.astype(jnp.bfloat16)
    grad_parts = grad_window.reshape(reach, tok_rows, 2 * kv_cols)[::-1]
    remaining = grad_parts
    held_count = reach
    for section_idx in range(reach.bit_length()):
        if held_count > 1:
            keep_count = (held_count + 1) // 2
            arrived = passed_along(remaining[keep_count:held_count], "ctx", -keep_count)
            moved_count = held_count - keep_count
            remaining = jnp.concatenate(
                [remaining[:moved_count] + arrived, remaining[moved_count:keep_count]], axis=0
            )
            held_count = keep_count
    summed = remaining[0]
    attended_out, grad_query_out, grad_keys_out, grad_values_out = (
        lax.all_to_all(
            attended_heads.reshape(tok_rows, group_width * kv_cols),
            "head",
            split_axis=0,
            concat_axis=1,
            tiled=True,
        ),
        lax.all_to_all(
            query_bf.reshape(tok_rows, group_width * kv_cols),
            "head",
            split_axis=0,
            concat_axis=1,
            tiled=True,
        ),
        lax.all_to_all(
            summed[:, :kv_cols].astype(jnp.bfloat16),
            "head",
            split_axis=0,
            concat_axis=1,
            tiled=True,
        ),
        lax.all_to_all(
            summed[:, kv_cols:].astype(jnp.bfloat16),
            "head",
            split_axis=0,
            concat_axis=1,
            tiled=True,
        ),
    )
    log_norm = log_total.reshape(kv_heads * group_width, tok_rows)
    return (attended_out, log_norm, grad_query_out, grad_keys_out, grad_values_out)


def solution(mesh):
    placed = (
        P(("ctx", "head"), None),
        P(("ctx", "head"), None),
        P(("ctx", "head"), None),
        P(("ctx", "head"), None),
        P(),
    )
    return jax.shard_map(
        on_device,
        mesh=mesh,
        in_specs=placed,
        out_specs=(
            P(("ctx", "head"), None),
            P("head", "ctx"),
            P(("ctx", "head"), None),
            P(("ctx", "head"), None),
            P(("ctx", "head"), None),
        ),
        check_vma=False,
    )
```

profile of v0, /device:TPU:13, one launch (start us, length us, event | category | flops | bytes accessed | tf_op | source)
XLA Modules:
  0.0 91.2 jit_solution(8681744121091855034)
XLA Ops:
  0.6 0.0 copy-start
  0.6 0.7 copy-done
  1.4 0.6 copy_bitcast_fusion.5
  2.0 3.9 %all-to-all-start = ((bf16[32,4,128]{2,0,1:T(8,128)(2,1)}), bf16[32,4,128]{2,0,1:T(8,128)(2,1)S(1)}, u32[]{:S(2)}, u32[]{:S(2)}) async-start(bf16[32,4,128]{2,0,1:T(8,128)(2,1)} %copy_bitcast_fusion.5), calls=%async_computation | async-start | bytes 65536 | tf_op jit(solution)/shard_map/all_to_all | solution.py:126
  5.9 1.4 %copy_bitcast_fusion.4 = bf16[32,4,128]{2,0,1:T(8,128)(2,1)} fusion(bf16[32,512]{1,0:T(8,128)(2,1)} %param.7), kind=kLoop, calls=%fused_computation.46 | loop fusion | bytes 65536 | tf_op jit(solution)/shard_map/all_to_all | solution.py:127
  7.3 0.8 reduce-window.8
  8.1 0.1 convert_reduce_fusion
  8.2 0.9 all-to-all-done
  9.1 4.0 %all-to-all-start.1 = ((bf16[32,4,128]{2,0,1:T(8,128)(2,1)}), bf16[32,4,128]{2,0,1:T(8,128)(2,1)S(1)}, u32[]{:S(2)}, u32[]{:S(2)}) async-start(bf16[32,4,128]{2,0,1:T(8,128)(2,1)} %copy_bitcast_fusion.4), calls=%async_computation.1 | async-start | bytes 65536 | tf_op jit(solution)/shard_map/all_to_all | solution.py:127
  13.1 0.1 convert_reduce_fusion.1
  13.2 1.7 %copy.128 = bf16[4,4,8,1024]{3,2,0,1:T(8,128)(2,1)} copy(bf16[4,4,8,1024]{3,2,1,0:T(8,128)(2,1)} %bitcast.166) | data formatting | bytes 524288 | tf_op jit(solution)/shard_map/all_to_all | solution.py:125
  14.9 1.4 %all-to-all-done.1 = bf16[32,4,128]{2,0,1:T(8,128)(2,1)S(1)} async-done(((bf16[32,4,128]{2,0,1:T(8,128)(2,1)}), bf16[32,4,128]{2,0,1:T(8,128)(2,1)S(1)}, u32[]{:S(2)}, u32[]{:S(2)}) %all-to-all-start.1) | async-done | bytes 32800 | tf_op jit(solution)/shard_map/all_to_all | solution.py:127
  16.3 4.2 %all-to-all-start.2 = ((bf16[32,4,1024]{2,0,1:T(8,128)(2,1)}), bf16[32,4,1024]{2,0,1:T(8,128)(2,1)S(1)}, u32[]{:S(2)}, u32[]{:S(2)}) async-start(bf16[32,4,1024]{2,0,1:T(8,128)(2,1)} %bitcast.147), calls=%async_computation.2 | async-start | bytes 524288 | tf_op jit(solution)/shard_map/all_to_all | solution.py:125
  20.4 3.1 %collective-permute-start = (bf16[128,256]{1,0:T(8,128)(2,1)S(1)}, bf16[128,256]{1,0:T(8,128)(2,1)S(1)}, u32[]{:S(2)}, u32[]{:S(2)}) collective-permute-start(bf16[128,256]{1,0:T(8,128)(2,1)S(1)} %pad_maximum_fusion.1), channel_id=1, source_target_pairs={{0,4},{4,8},{8,12},{12,16},{16,20},{20,24},{24,28},{1,5},{5,9},{9,... | collective-permute-start | bytes 196616 | tf_op jit(solution)/shard_map/ppermute | solution.py:17
  23.6 1.7 %copy.127 = bf16[4,4,8,1024]{3,2,0,1:T(8,128)(2,1)} copy(bf16[4,4,8,1024]{3,2,1,0:T(8,128)(2,1)} %bitcast.167) | data formatting | bytes 524288 | tf_op jit(solution)/shard_map/all_to_all | solution.py:128
  25.3 0.7 collective-permute-done
  26.0 3.2 %collective-permute-start.1 = (bf16[256,256]{1,0:T(8,128)(2,1)S(1)}, bf16[256,256]{1,0:T(8,128)(2,1)S(1)}, u32[]{:S(2)}, u32[]{:S(2)}) collective-permute-start(bf16[256,256]{1,0:T(8,128)(2,1)S(1)} %maximum_maximum_fusion.1), channel_id=1, source_target_pairs={{0,8},{4,12},{8,16},{12,20},{16,24},{20,28},{1,9},{5,13},{9,17},{1... | collective-permute-start | bytes 393224 | tf_op jit(solution)/shard_map/ppermute | solution.py:17
  29.2 0.0 all-to-all-done.2
  29.3 4.5 %all-to-all-start.4 = ((bf16[32,4,1024]{2,0,1:T(8,128)(2,1)}), bf16[32,4,1024]{2,0,1:T(8,128)(2,1)S(1)}, u32[]{:S(2)}, u32[]{:S(2)}) async-start(bf16[32,4,1024]{2,0,1:T(8,128)(2,1)} %bitcast.146), calls=%async_computation.4 | async-start | bytes 524288 | tf_op jit(solution)/shard_map/all_to_all | solution.py:128
  33.8 0.2 compare_and_fusion
  34.0 4.9 %all-to-all-done.4 = bf16[32,4,1024]{2,0,1:T(8,128)(2,1)S(1)} async-done(((bf16[32,4,1024]{2,0,1:T(8,128)(2,1)}), bf16[32,4,1024]{2,0,1:T(8,128)(2,1)S(1)}, u32[]{:S(2)}, u32[]{:S(2)}) %all-to-all-start.4) | async-done | bytes 262176 | tf_op jit(solution)/shard_map/all_to_all | solution.py:128
  39.0 0.0 collective-permute-done.1
  39.0 0.5 fusion.3
  39.5 0.4 fusion.6
  40.0 0.0 copy-start.1
  40.0 0.5 fusion.9
  40.4 0.3 bitcast_convert_fusion
  40.8 0.0 copy-done.1
  40.8 0.2 copy.89
  41.0 0.2 multiply_reduce_fusion
  41.3 0.5 fusion.2
  41.8 0.5 convolution_bitcast_fusion.1
  42.3 0.5 convolution_bitcast_fusion
  42.9 2.1 %collective-permute-start.2 = (f32[2,128,256]{1,2,0:T(8,128)S(1)}, f32[2,128,256]{1,2,0:T(8,128)S(1)}, u32[]{:S(2)}, u32[]{:S(2)}) collective-permute-start(f32[2,128,256]{1,2,0:T(8,128)S(1)} %slice.45), channel_id=1, source_target_pairs={{8,0},{12,4},{16,8},{20,12},{24,16},{28,20},{9,1},{13,5},{17,9},{2... | collective-permute-start | bytes 786440 | tf_op jit(solution)/shard_map/ppermute | solution.py:17
  44.9 6.7 %collective-permute-done.2 = f32[2,128,256]{1,2,0:T(8,128)S(1)} collective-permute-done((f32[2,128,256]{1,2,0:T(8,128)S(1)}, f32[2,128,256]{1,2,0:T(8,128)S(1)}, u32[]{:S(2)}, u32[]{:S(2)}) %collective-permute-start.2) | collective-permute-done | bytes 262176 | tf_op jit(solution)/shard_map/ppermute | solution.py:17
  51.7 3.0 %collective-permute-start.3 = (f32[1,128,256]{1,2,0:T(8,128)S(1)}, f32[1,128,256]{1,2,0:T(8,128)S(1)}, u32[]{:S(2)}, u32[]{:S(2)}) collective-permute-start(f32[1,128,256]{1,2,0:T(8,128)S(1)} %slice.55), channel_id=1, source_target_pairs={{4,0},{8,4},{12,8},{16,12},{20,16},{24,20},{28,24},{5,1},{9,5},{13... | collective-permute-start | bytes 393224 | tf_op jit(solution)/shard_map/ppermute | solution.py:17
  54.8 0.3 fusion.10
  55.1 0.2 copy.74
  55.3 0.8 all_to_all.126
  56.1 5.4 %all-to-all-start.5 = ((bf16[4,32,1024]{2,1,0:T(8,128)(2,1)}), bf16[4,32,1024]{2,1,0:T(8,128)(2,1)S(1)}, u32[]{:S(2)}, u32[]{:S(2)}) async-start(bf16[4,32,1024]{2,1,0:T(8,128)(2,1)} %all_to_all.126), calls=%async_computation.5 | async-start | bytes 524288 | tf_op jit(solution)/shard_map/all_to_all | solution.py:173
  61.6 0.2 copy.68
  61.8 0.8 all_to_all.119
  62.6 0.0 collective-permute-done.3
  62.6 4.1 %all-to-all-done.5 = bf16[4,32,1024]{2,1,0:T(8,128)(2,1)S(1)} async-done(((bf16[4,32,1024]{2,1,0:T(8,128)(2,1)}), bf16[4,32,1024]{2,1,0:T(8,128)(2,1)S(1)}, u32[]{:S(2)}, u32[]{:S(2)}) %all-to-all-start.5) | async-done | bytes 262176 | tf_op jit(solution)/shard_map/all_to_all | solution.py:173
  66.7 4.2 %all-to-all-start.3 = ((bf16[4,32,1024]{2,1,0:T(8,128)(2,1)}), bf16[4,32,1024]{2,1,0:T(8,128)(2,1)S(1)}, u32[]{:S(2)}, u32[]{:S(2)}) async-start(bf16[4,32,1024]{2,1,0:T(8,128)(2,1)} %all_to_all.119), calls=%async_computation.3 | async-start | bytes 524288 | tf_op jit(solution)/shard_map/all_to_all | solution.py:166
  71.0 0.7 copy.80
  71.7 4.4 %all-to-all-done.3 = bf16[4,32,1024]{2,1,0:T(8,128)(2,1)S(1)} async-done(((bf16[4,32,1024]{2,1,0:T(8,128)(2,1)}), bf16[4,32,1024]{2,1,0:T(8,128)(2,1)S(1)}, u32[]{:S(2)}, u32[]{:S(2)}) %all-to-all-start.3) | async-done | bytes 262176 | tf_op jit(solution)/shard_map/all_to_all | solution.py:166
  76.2 4.1 %all-to-all-start.7 = ((bf16[4,32,128]{2,1,0:T(8,128)(2,1)}), bf16[4,32,128]{2,1,0:T(8,128)(2,1)S(1)}, u32[]{:S(2)}, u32[]{:S(2)}) async-start(bf16[4,32,128]{2,1,0:T(8,128)(2,1)} %bitcast.42), calls=%async_computation.7 | async-start | bytes 65536 | tf_op jit(solution)/shard_map/all_to_all | solution.py:187
  80.3 0.7 copy.106
  81.0 0.7 copy.105
  81.7 0.7 copy.78
  82.4 1.0 %all-to-all-done.7 = bf16[4,32,128]{2,1,0:T(8,128)(2,1)S(1)} async-done(((bf16[4,32,128]{2,1,0:T(8,128)(2,1)}), bf16[4,32,128]{2,1,0:T(8,128)(2,1)S(1)}, u32[]{:S(2)}, u32[]{:S(2)}) %all-to-all-start.7) | async-done | bytes 32800 | tf_op jit(solution)/shard_map/all_to_all | solution.py:187
  83.4 4.0 %all-to-all-start.6 = ((bf16[4,32,128]{2,1,0:T(8,128)(2,1)}), bf16[4,32,128]{2,1,0:T(8,128)(2,1)S(1)}, u32[]{:S(2)}, u32[]{:S(2)}) async-start(bf16[4,32,128]{2,1,0:T(8,128)(2,1)} %bitcast.40), calls=%async_computation.6 | async-start | bytes 65536 | tf_op jit(solution)/shard_map/all_to_all | solution.py:180
  87.4 0.6 copy_bitcast_fusion.2
  88.1 2.6 %all-to-all-done.6 = bf16[4,32,128]{2,1,0:T(8,128)(2,1)S(1)} async-done(((bf16[4,32,128]{2,1,0:T(8,128)(2,1)}), bf16[4,32,128]{2,1,0:T(8,128)(2,1)S(1)}, u32[]{:S(2)}, u32[]{:S(2)}) %all-to-all-start.6) | async-done | bytes 32800 | tf_op jit(solution)/shard_map/all_to_all | solution.py:180
  90.6 0.6 copy_bitcast_fusion.3
  (18 shorter events, 0.3 us)
Async XLA Ops:
  0.6 0.8 copy-start
  2.0 7.1 %all-to-all-start = ((bf16[32,4,128]{2,0,1:T(8,128)(2,1)}), bf16[32,4,128]{2,0,1:T(8,128)(2,1)S(1)}, u32[]{:S(2)}, u32[]{:S(2)}) async-start(bf16[32,4,128]{2,0,1:T(8,128)(2,1)} %copy_bitcast_fusion.5), calls=%async_computation | async-start | bytes 65536 | tf_op jit(solution)/shard_map/all_to_all | solution.py:126
  9.1 7.2 %all-to-all-start.1 = ((bf16[32,4,128]{2,0,1:T(8,128)(2,1)}), bf16[32,4,128]{2,0,1:T(8,128)(2,1)S(1)}, u32[]{:S(2)}, u32[]{:S(2)}) async-start(bf16[32,4,128]{2,0,1:T(8,128)(2,1)} %copy_bitcast_fusion.4), calls=%async_computation.1 | async-start | bytes 65536 | tf_op jit(solution)/shard_map/all_to_all | solution.py:127
  16.3 13.0 %all-to-all-start.2 = ((bf16[32,4,1024]{2,0,1:T(8,128)(2,1)}), bf16[32,4,1024]{2,0,1:T(8,128)(2,1)S(1)}, u32[]{:S(2)}, u32[]{:S(2)}) async-start(bf16[32,4,1024]{2,0,1:T(8,128)(2,1)} %bitcast.147), calls=%async_computation.2 | async-start | bytes 524288 | tf_op jit(solution)/shard_map/all_to_all | solution.py:125
  20.4 5.6 %collective-permute-start = (bf16[128,256]{1,0:T(8,128)(2,1)S(1)}, bf16[128,256]{1,0:T(8,128)(2,1)S(1)}, u32[]{:S(2)}, u32[]{:S(2)}) collective-permute-start(bf16[128,256]{1,0:T(8,128)(2,1)S(1)} %pad_maximum_fusion.1), channel_id=1, source_target_pairs={{0,4},{4,8},{8,12},{12,16},{16,20},{20,24},{24,28},{1,5},{5,9},{9,... | collective-permute-start | bytes 196616 | tf_op jit(solution)/shard_map/ppermute | solution.py:17
  26.0 12.9 %collective-permute-start.1 = (bf16[256,256]{1,0:T(8,128)(2,1)S(1)}, bf16[256,256]{1,0:T(8,128)(2,1)S(1)}, u32[]{:S(2)}, u32[]{:S(2)}) collective-permute-start(bf16[256,256]{1,0:T(8,128)(2,1)S(1)} %maximum_maximum_fusion.1), channel_id=1, source_target_pairs={{0,8},{4,12},{8,16},{12,20},{16,24},{20,28},{1,9},{5,13},{9,17},{1... | collective-permute-start | bytes 393224 | tf_op jit(solution)/shard_map/ppermute | solution.py:17
  29.3 9.7 %all-to-all-start.4 = ((bf16[32,4,1024]{2,0,1:T(8,128)(2,1)}), bf16[32,4,1024]{2,0,1:T(8,128)(2,1)S(1)}, u32[]{:S(2)}, u32[]{:S(2)}) async-start(bf16[32,4,1024]{2,0,1:T(8,128)(2,1)} %bitcast.146), calls=%async_computation.4 | async-start | bytes 524288 | tf_op jit(solution)/shard_map/all_to_all | solution.py:128
  40.0 0.8 copy-start.1
  42.9 8.8 %collective-permute-start.2 = (f32[2,128,256]{1,2,0:T(8,128)S(1)}, f32[2,128,256]{1,2,0:T(8,128)S(1)}, u32[]{:S(2)}, u32[]{:S(2)}) collective-permute-start(f32[2,128,256]{1,2,0:T(8,128)S(1)} %slice.45), channel_id=1, source_target_pairs={{8,0},{12,4},{16,8},{20,12},{24,16},{28,20},{9,1},{13,5},{17,9},{2... | collective-permute-start | bytes 786440 | tf_op jit(solution)/shard_map/ppermute | solution.py:17
  51.7 10.8 %collective-permute-start.3 = (f32[1,128,256]{1,2,0:T(8,128)S(1)}, f32[1,128,256]{1,2,0:T(8,128)S(1)}, u32[]{:S(2)}, u32[]{:S(2)}) collective-permute-start(f32[1,128,256]{1,2,0:T(8,128)S(1)} %slice.55), channel_id=1, source_target_pairs={{4,0},{8,4},{12,8},{16,12},{20,16},{24,20},{28,24},{5,1},{9,5},{13... | collective-permute-start | bytes 393224 | tf_op jit(solution)/shard_map/ppermute | solution.py:17
  56.1 10.6 %all-to-all-start.5 = ((bf16[4,32,1024]{2,1,0:T(8,128)(2,1)}), bf16[4,32,1024]{2,1,0:T(8,128)(2,1)S(1)}, u32[]{:S(2)}, u32[]{:S(2)}) async-start(bf16[4,32,1024]{2,1,0:T(8,128)(2,1)} %all_to_all.126), calls=%async_computation.5 | async-start | bytes 524288 | tf_op jit(solution)/shard_map/all_to_all | solution.py:173
  66.7 9.4 %all-to-all-start.3 = ((bf16[4,32,1024]{2,1,0:T(8,128)(2,1)}), bf16[4,32,1024]{2,1,0:T(8,128)(2,1)S(1)}, u32[]{:S(2)}, u32[]{:S(2)}) async-start(bf16[4,32,1024]{2,1,0:T(8,128)(2,1)} %all_to_all.119), calls=%async_computation.3 | async-start | bytes 524288 | tf_op jit(solution)/shard_map/all_to_all | solution.py:166
  76.2 7.3 %all-to-all-start.7 = ((bf16[4,32,128]{2,1,0:T(8,128)(2,1)}), bf16[4,32,128]{2,1,0:T(8,128)(2,1)S(1)}, u32[]{:S(2)}, u32[]{:S(2)}) async-start(bf16[4,32,128]{2,1,0:T(8,128)(2,1)} %bitcast.42), calls=%async_computation.7 | async-start | bytes 65536 | tf_op jit(solution)/shard_map/all_to_all | solution.py:187
  83.4 7.2 %all-to-all-start.6 = ((bf16[4,32,128]{2,1,0:T(8,128)(2,1)}), bf16[4,32,128]{2,1,0:T(8,128)(2,1)S(1)}, u32[]{:S(2)}, u32[]{:S(2)}) async-start(bf16[4,32,128]{2,1,0:T(8,128)(2,1)} %bitcast.40), calls=%async_computation.6 | async-start | bytes 65536 | tf_op jit(solution)/shard_map/all_to_all | solution.py:180
where the time goes:
time: 92.7 us; the launch traced here: 91.2 us
  starting transfers between devices  45.8 us (49%)
  waiting for transfers between devices  26.8 us (29%)
  local copies, waits for them, and re-layouts  12.6 us (14%)
  matrix products  2.6 us (3%)
  other arithmetic  2.46 us (3%)
    ppermute x4, starting transfers between devices, passed_along(): return lax.ppermute(value, axis, pairs)  11.5 us
    ppermute x4, waiting for transfers between devices, passed_along(): return lax.ppermute(value, axis, pairs)  7.47 us
    all_to_all x1, starting transfers between devices, on_device(): lax.all_to_all(query_bf.reshape(tok_rows, group_width * kv_cols), 'head',...  5.44 us
    all_to_all x1, waiting for transfers between devices, on_device(): lax.all_to_all(output_gradient, 'head', split_axis=1, concat_axis=0, tile...  4.91 us
    all_to_all x1, starting transfers between devices, on_device(): lax.all_to_all(output_gradient, 'head', split_axis=1, concat_axis=0, tile...  4.5 us
    all_to_all x1, waiting for transfers between devices, on_device(): lax.all_to_all(attended_heads.reshape(tok_rows, group_width * kv_cols), '...  4.44 us
    all_to_all x1, starting transfers between devices, on_device(): lax.all_to_all(attended_heads.reshape(tok_rows, group_width * kv_cols), '...  4.25 us
    all_to_all x1, starting transfers between devices, on_device(): lax.all_to_all(queries, 'head', split_axis=1, concat_axis=0, tiled=True)  4.15 us
  transfers between devices with their start and end apart: 12, of which 9 were waited for; matrix products, arithmetic and copies ran while one was open for 11% of the time, Pallas kernels for 0%

commit v1 on v0

v1 whole, which is shorter than its diff:
```python
import functools
import math

import jax
import jax.numpy as jnp
from jax import lax
from jax.experimental import pallas as pl
from jax.experimental.pallas import tpu as pltpu
from jax.sharding import PartitionSpec as P

WIDTH = 128
MESH = pl.DeviceIdType.MESH
FILL = -1e30
NT = (((1,), (1,)), ((), ()))
TN = (((0,), (0,)), ((), ()))
NN = (((1,), (0,)), ((), ()))


def dot(a, b, dims):
    return lax.dot_general(a, b, dims, preferred_element_type=jnp.float32)


def kernel(
    ctxs,
    heads,
    reach,
    q_ref,
    k_ref,
    v_ref,
    g_ref,
    doc_ref,
    att_out,
    norm_out,
    dq_out,
    dk_out,
    dv_out,
    q_buf,
    g_buf,
    kv_buf,
    bias,
    probs,
    dscores,
    att_buf,
    dq_buf,
    dkv_own,
    dkv_send,
    dkv_recv,
    dkv_fin,
    norm_buf,
    in_send,
    in_recv,
    ctx_send,
    ctx_recv,
    out_send,
    out_recv,
    back_send,
    back_recv,
    local_sem,
):
    u = lax.axis_index("ctx")
    g = lax.axis_index("head")
    tok = q_ref.shape[0]
    block = tok * heads
    group_cols = q_ref.shape[1] // heads
    per_group = group_cols // WIDTH
    window = reach * block
    scale = 1.0 / math.sqrt(WIDTH)
    last = reach - 1

    def rows(i):
        return pl.ds(pl.multiple_of(i * tok, tok), tok)

    def cols(i, width):
        return pl.ds(pl.multiple_of(i * width, width), width)

    barrier = pltpu.get_barrier_semaphore()
    for d in range(1, heads):
        pl.semaphore_signal(
            barrier, inc=1, device_id=(u, lax.rem(g + d, heads)), device_id_type=MESH
        )
    for k in range(1, reach):
        @pl.when(u + k < ctxs)
        def _():
            pl.semaphore_signal(barrier, inc=1, device_id=(u + k, g), device_id_type=MESH)

        @pl.when(u - k >= 0)
        def _():
            pl.semaphore_signal(barrier, inc=1, device_id=(u - k, g), device_id_type=MESH)

    own = [
        (k_ref.at[:, cols(g, WIDTH)], kv_buf.at[last, rows(g), pl.ds(0, WIDTH)]),
        (v_ref.at[:, cols(g, WIDTH)], kv_buf.at[last, rows(g), pl.ds(WIDTH, WIDTH)]),
        (q_ref.at[:, cols(g, group_cols)], q_buf.at[rows(g), :]),
        (g_ref.at[:, cols(g, group_cols)], g_buf.at[rows(g), :]),
    ]
    own_copies = [
        pltpu.make_async_copy(src, dst, local_sem.at[i]) for i, (src, dst) in enumerate(own)
    ]
    for copy in own_copies:
        copy.start()

    for k in range(1, reach):
        @pl.when(u - k < 0)
        def _():
            kv_buf[last - k] = jnp.zeros((block, 2 * WIDTH), jnp.bfloat16)

        @pl.when(u + k >= ctxs)
        def _():
            dkv_recv[k - 1] = jnp.zeros((block, 2 * WIDTH), jnp.bfloat16)

    pl.semaphore_wait(
        barrier,
        (heads - 1) + jnp.minimum(u, reach - 1) + jnp.minimum(ctxs - 1 - u, reach - 1),
    )

    def in_src(kind, i):
        ref = (k_ref, v_ref, q_ref, g_ref)[kind]
        return ref.at[:, cols(i, WIDTH if kind < 2 else group_cols)]

    def in_dst(kind, i):
        if kind < 2:
            return kv_buf.at[last, rows(i), pl.ds(kind * WIDTH, WIDTH)]
        return (q_buf, g_buf)[kind - 2].at[rows(i), :]

    def in_copy(kind, d):
        peer = lax.rem(g + d, heads)
        return pltpu.make_async_remote_copy(
            src_ref=in_src(kind, peer),
            dst_ref=in_dst(kind, g),
            send_sem=in_send.at[kind, d - 1],
            recv_sem=in_recv.at[kind, d - 1],
            device_id=(u, peer),
            device_id_type=MESH,
        )

    def in_arrival(kind, d):
        peer = lax.rem(g + heads - d, heads)
        return pltpu.make_async_remote_copy(
            src_ref=in_dst(kind, peer),
            dst_ref=in_dst(kind, peer),
            send_sem=in_send.at[kind, d - 1],
            recv_sem=in_recv.at[kind, d - 1],
            device_id=(u, peer),
            device_id_type=MESH,
        )

    for kind in range(4):
        for d in range(1, heads):
            in_copy(kind, d).start()

    query_pos = u * block + lax.broadcasted_iota(jnp.int32, (1, block), 1)
    begins = jnp.zeros((1, block), jnp.int32)
    bound = jnp.int32(0)
    for j in range(doc_ref.shape[0]):
        bound = bound + doc_ref[j]
        begins = jnp.where(query_pos >= bound, bound, begins)
    key_pos = (u - last) * block + lax.broadcasted_iota(jnp.int32, (window, block), 0)
    bias[...] = jnp.where((key_pos >= begins) & (key_pos <= query_pos), 0.0, FILL)

    own_copies[0].wait()
    own_copies[1].wait()
    for kind in range(2):
        for d in range(1, heads):
            in_arrival(kind, d).wait_recv()

    def ctx_copy(k, to):
        return pltpu.make_async_remote_copy(
            src_ref=kv_buf.at[last],
            dst_ref=kv_buf.at[last - k],
            send_sem=ctx_send.at[k - 1],
            recv_sem=ctx_recv.at[k - 1],
            device_id=(to, g),
            device_id_type=MESH,
        )

    for k in range(1, reach):
        @pl.when(u + k < ctxs)
        def _():
            ctx_copy(k, u + k).start()

    own_copies[2].wait()
    for d in range(1, heads):
        in_arrival(2, d).wait_recv()
    for k in range(1, reach):
        @pl.when(u - k >= 0)
        def _():
            ctx_copy(k, u - k).wait_recv()

    keys = kv_buf[:, :, :WIDTH].reshape(window, WIDTH)
    values = kv_buf[:, :, WIDTH:].reshape(window, WIDTH)

    factor = scale * math.log2(math.e)
    for h in range(per_group):
        at = slice(h * WIDTH, (h + 1) * WIDTH)
        scores = dot(keys, q_buf[:, at], NT) + bias[...]
        top = jnp.max(scores, axis=0, keepdims=True)
        weights = jnp.exp2((scores - top) * factor)
        total = jnp.sum(weights, axis=0, keepdims=True)
        norm_buf[h : h + 1, :] = top * scale + jnp.log(total)
        p = (weights * (1.0 / total)).astype(jnp.bfloat16)
        probs[:, h * block : (h + 1) * block] = p
        att_buf[:, at] = dot(p, values, TN).astype(jnp.bfloat16)

    def out_src(kind, i):
        if kind < 2:
            return (att_buf, dq_buf)[kind].at[rows(i), :]
        return dkv_fin.at[rows(i), pl.ds((kind - 2) * WIDTH, WIDTH)]

    def out_dst(kind, i):
        ref = (att_out, dq_out, dk_out, dv_out)[kind]
        return ref.at[:, cols(i, WIDTH if kind >= 2 else group_cols)]

    def out_copy(kind, d):
        peer = lax.rem(g + d, heads)
        return pltpu.make_async_remote_copy(
            src_ref=out_src(kind, peer),
            dst_ref=out_dst(kind, g),
            send_sem=out_send.at[kind, d - 1],
            recv_sem=out_recv.at[kind, d - 1],
            device_id=(u, peer),
            device_id_type=MESH,
        )

    def out_arrival(kind, d):
        peer = lax.rem(g + heads - d, heads)
        return pltpu.make_async_remote_copy(
            src_ref=out_dst(kind, peer),
            dst_ref=out_dst(kind, peer),
            send_sem=out_send.at[kind, d - 1],
            recv_sem=out_recv.at[kind, d - 1],
            device_id=(u, peer),
            device_id_type=MESH,
        )

    def own_out(kind):
        return pltpu.make_async_copy(out_src(kind, g), out_dst(kind, g), local_sem.at[4 + kind])

    def send_out(kind):
        for d in range(1, heads):
            out_copy(kind, d).start()
        own_out(kind).start()

    send_out(0)
    norm_copy = pltpu.make_async_copy(norm_buf, norm_out, local_sem.at[8])
    norm_copy.start()

    own_copies[3].wait()
    for d in range(1, heads):
        in_arrival(3, d).wait_recv()

    for h in range(per_group):
        at = slice(h * WIDTH, (h + 1) * WIDTH)
        grad_probs = dot(values, g_buf[:, at], NT)
        p = probs[:, h * block : (h + 1) * block].astype(jnp.float32)
        delta = jnp.sum(p * grad_probs, axis=0, keepdims=True)
        dscores[:, h * block : (h + 1) * block] = (p * (grad_probs - delta) * scale).astype(
            jnp.bfloat16
        )

    def stacked(ref):
        return jnp.concatenate(
            [ref[:, h * WIDTH : (h + 1) * WIDTH] for h in range(per_group)], axis=0
        )

    queries = stacked(q_buf)
    grads = stacked(g_buf)

    def back_copy(k, to):
        return pltpu.make_async_remote_copy(
            src_ref=dkv_send.at[k - 1],
            dst_ref=dkv_recv.at[k - 1],
            send_sem=back_send.at[k - 1],
            recv_sem=back_recv.at[k - 1],
            device_id=(to, g),
            device_id_type=MESH,
        )

    for k in range(reach - 1, -1, -1):
        part = slice((last - k) * block, (last - k + 1) * block)
        dk = dot(dscores[part, :], queries, NN)
        dv = dot(probs[part, :], grads, NN)
        if k == 0:
            dkv_own[:, :WIDTH] = dk
            dkv_own[:, WIDTH:] = dv
        else:
            dkv_send[k - 1, :, :WIDTH] = dk.astype(jnp.bfloat16)
            dkv_send[k - 1, :, WIDTH:] = dv.astype(jnp.bfloat16)

            @pl.when(u - k >= 0)
            def _():
                back_copy(k, u - k).start()

    for h in range(per_group):
        at = slice(h * WIDTH, (h + 1) * WIDTH)
        ds = dscores[:, h * block : (h + 1) * block]
        dq_buf[:, at] = dot(ds, keys, TN).astype(jnp.bfloat16)
    send_out(1)

    for k in range(1, reach):
        @pl.when(u + k < ctxs)
        def _():
            back_copy(k, u + k).wait_recv()

    total = dkv_own[...]
    for k in range(1, reach):
        total = total + dkv_recv[k - 1].astype(jnp.float32)
    dkv_fin[...] = total.astype(jnp.bfloat16)
    send_out(2)
    send_out(3)

    for kind in range(4):
        for d in range(1, heads):
            in_copy(kind, d).wait_send()
    for k in range(1, reach):
        @pl.when(u + k < ctxs)
        def _():
            ctx_copy(k, u + k).wait_send()

        @pl.when(u - k >= 0)
        def _():
            back_copy(k, u - k).wait_send()

    norm_copy.wait()
    for kind in range(4):
        own_out(kind).wait()
        for d in range(1, heads):
            out_copy(kind, d).wait_send()
            out_arrival(kind, d).wait_recv()


def solution(mesh):
    ctxs, heads = mesh.shape["ctx"], mesh.shape["head"]
    reach = min(16, ctxs // 2)

    def step(q, k, v, g, doc_lengths):
        tok = q.shape[0]
        block = tok * heads
        group_cols = q.shape[1] // heads
        per_group = group_cols // WIDTH
        window = reach * block
        bf16, f32 = jnp.bfloat16, jnp.float32
        hbm = pl.BlockSpec(memory_space=pl.ANY)
        dma = pltpu.SemaphoreType.DMA
        return pl.pallas_call(
            functools.partial(kernel, ctxs, heads, reach),
            out_shape=(
                jax.ShapeDtypeStruct(q.shape, bf16),
                jax.ShapeDtypeStruct((per_group, block), f32),
                jax.ShapeDtypeStruct(q.shape, bf16),
                jax.ShapeDtypeStruct(k.shape, bf16),
                jax.ShapeDtypeStruct(k.shape, bf16),
            ),
            in_specs=[hbm] * 4 + [pl.BlockSpec(memory_space=pltpu.SMEM)],
            out_specs=(hbm,) * 5,
            scratch_shapes=[
                pltpu.VMEM((block, group_cols), bf16),
                pltpu.VMEM((block, group_cols), bf16),
                pltpu.VMEM((reach, block, 2 * WIDTH), bf16),
                pltpu.VMEM((window, block), f32),
                pltpu.VMEM((window, per_group * block), bf16),
                pltpu.VMEM((window, per_group * block), bf16),
                pltpu.VMEM((block, group_cols), bf16),
                pltpu.VMEM((block, group_cols), bf16),
                pltpu.VMEM((block, 2 * WIDTH), f32),
                pltpu.VMEM((reach - 1, block, 2 * WIDTH), bf16),
                pltpu.VMEM((reach - 1, block, 2 * WIDTH), bf16),
                pltpu.VMEM((block, 2 * WIDTH), bf16),
                pltpu.VMEM((per_group, block), f32),
                dma((4, heads - 1)),
                dma((4, heads - 1)),
                dma((reach - 1,)),
                dma((reach - 1,)),
                dma((4, heads - 1)),
                dma((4, heads - 1)),
                dma((reach - 1,)),
                dma((reach - 1,)),
                dma((9,)),
            ],
            compiler_params=pltpu.CompilerParams(
                collective_id=0, has_side_effects=True, vmem_limit_bytes=40 * 1024 * 1024
            ),
        )(q, k, v, g, doc_lengths)

    placed = P(("ctx", "head"), None)
    return jax.shard_map(
        step,
        mesh=mesh,
        in_specs=(placed,) * 4 + (P(),),
        out_specs=(placed, P("head", "ctx"), placed, placed, placed),
        check_vma=False,
    )
```

time: 92.7 us -> 35.2 us (0.38); the launches traced: 91.2 us -> 34.9 us
  starting transfers between devices: 45.8 us -> 0 us
  Pallas kernels: 0 us -> 26.9 us
  waiting for transfers between devices: 26.8 us -> 0 us
  local copies, waits for them, and re-layouts: 12.6 us -> 7.29 us
  matrix products: 2.6 us -> 0 us
  other arithmetic: 2.46 us -> 0 us
    all_to_all x8 -> x0, starting transfers between devices: 34.4 us -> none  [the longest x1 5.44 us: on_device(): lax.all_to_all(query_bf.reshape(tok_rows, group_width * kv_cols), 'head',...]
    pallas_call x0 -> x1, Pallas kernels: none -> 26.9 us  [step(): pl.pallas_call(functools.partial(kernel, ctxs, heads, reach), out_shape=(...]
    all_to_all x8 -> x0, waiting for transfers between devices: 19.3 us -> none  [the longest x1 4.91 us: on_device(): lax.all_to_all(output_gradient, 'head', split_axis=1, concat_axis=0, tile...]
    ppermute x4 -> x0, starting transfers between devices: 11.5 us -> none  [passed_along(): return lax.ppermute(value, axis, pairs)]
    all_to_all x10 -> x0, local copies, waits for them, and re-layouts: 9.65 us -> none  [the longest x1 1.67 us: on_device(): lax.all_to_all(output_gradient, 'head', split_axis=1, concat_axis=0, tile...]
    ppermute x4 -> x0, waiting for transfers between devices: 7.47 us -> none  [passed_along(): return lax.ppermute(value, axis, pairs)]
    unnamed x7 -> x15, local copies, waits for them, and re-layouts: 1.08 us -> 7.29 us
    dot_general x6 -> x0, matrix products: 2.6 us -> none  [the longest x1 0.52 us: grad_step(): jnp.einsum('pgjd,kgd->gjpk', grad_heads, block_of_values, preferred_eleme...]
  transfers between devices with their start and end apart: 12 -> 0, of which waited for: 9 -> 0; matrix products, arithmetic and copies ran while one was open for 11% -> 0% of each run, Pallas kernels for 0% -> 0%
where the time goes in v1:
time: 35.2 us; the launch traced here: 34.9 us
  Pallas kernels  26.9 us (76%)
  local copies, waits for them, and re-layouts  7.29 us (21%)
  between operations  0.66 us (2%)
    pallas_call x1, Pallas kernels, step(): pl.pallas_call(functools.partial(kernel, ctxs, heads, reach), out_shape=(...  26.9 us
    unnamed x15, local copies, waits for them, and re-layouts  7.29 us

profile of v1, /device:TPU:13, one launch (start us, length us, event | category | flops | bytes accessed | tf_op | source)
XLA Modules:
  0.0 34.9 jit_solution(9888549308108200282)
XLA Ops:
  0.6 0.0 copy-start
  0.6 0.9 %copy-done = bf16[32,4096]{1,0:T(8,128)(2,1)S(1)} copy-done((bf16[32,4096]{1,0:T(8,128)(2,1)S(1)}, bf16[32,4096]{1,0:T(8,128)(2,1)}, u32[]{:S(2)}) %copy-start) | copy-done | bytes 262168
  1.6 0.0 copy-start.1
  1.6 0.9 %copy-done.1 = bf16[32,4096]{1,0:T(8,128)(2,1)S(1)} copy-done((bf16[32,4096]{1,0:T(8,128)(2,1)S(1)}, bf16[32,4096]{1,0:T(8,128)(2,1)}, u32[]{:S(2)}) %copy-start.1) | copy-done | bytes 262168
  2.5 0.0 copy-start.2
  2.5 0.8 %copy-done.2 = bf16[32,512]{1,0:T(8,128)(2,1)S(1)} copy-done((bf16[32,512]{1,0:T(8,128)(2,1)S(1)}, bf16[32,512]{1,0:T(8,128)(2,1)}, u32[]{:S(2)}) %copy-start.2) | copy-done | bytes 32792
  3.3 0.0 copy-start.3
  3.3 0.8 %copy-done.3 = bf16[32,512]{1,0:T(8,128)(2,1)S(1)} copy-done((bf16[32,512]{1,0:T(8,128)(2,1)S(1)}, bf16[32,512]{1,0:T(8,128)(2,1)}, u32[]{:S(2)}) %copy-start.3) | copy-done | bytes 32792
  4.1 0.0 copy-start.4
  4.1 0.7 %copy-done.4 = s32[4]{0:T(128)S(1)} copy-done((s32[4]{0:T(128)S(1)}, s32[4]{0:T(128)}, u32[]{:S(2)}) %copy-start.4) | copy-done | bytes 40
  4.7 26.9 %shard_map.92 = (bf16[32,4096]{1,0:T(8,128)(2,1)S(1)}, f32[8,128]{1,0:T(8,128)S(1)}, bf16[32,4096]{1,0:T(8,128)(2,1)S(1)}, bf16[32,512]{1,0:T(8,128)(2,1)S(1)}, bf16[32,512]{1,0:T(8,128)(2,1)S(1)}) custom-call(bf16[32,4096]{1,0:T(8,128)(2,1)S(1)} %copy-done, bf16[32,512]{1,0:T(8,128)(2,1)S(1)} %copy-done.2, bf16[32,512]{1,0:T(8,128)(2,1)S(1)} %copy-done.3, ...), custom_call_target="tpu_custom_call" | custom-call | tf_op jit(solution)/shard_map/pallas_call | solution.py:344
  31.7 0.7 %copy.15 = bf16[32,4096]{1,0:T(8,128)(2,1)} copy(bf16[32,4096]{1,0:T(8,128)(2,1)S(1)} %get-tuple-element.10) | data formatting | bytes 524288
  32.4 0.6 %copy.16 = f32[8,128]{1,0:T(8,128)} copy(f32[8,128]{1,0:T(8,128)S(1)} %get-tuple-element.11) | data formatting | bytes 8192
  33.0 0.7 %copy.17 = bf16[32,4096]{1,0:T(8,128)(2,1)} copy(bf16[32,4096]{1,0:T(8,128)(2,1)S(1)} %get-tuple-element.12) | data formatting | bytes 524288
  33.7 0.6 %copy.18 = bf16[32,512]{1,0:T(8,128)(2,1)} copy(bf16[32,512]{1,0:T(8,128)(2,1)S(1)} %get-tuple-element.13) | data formatting | bytes 65536
  34.3 0.6 %copy.19 = bf16[32,512]{1,0:T(8,128)(2,1)} copy(bf16[32,512]{1,0:T(8,128)(2,1)S(1)} %get-tuple-element.14) | data formatting | bytes 65536
Async XLA Ops:
  0.6 1.0 %copy-start = (bf16[32,4096]{1,0:T(8,128)(2,1)S(1)}, bf16[32,4096]{1,0:T(8,128)(2,1)}, u32[]{:S(2)}) copy-start(bf16[32,4096]{1,0:T(8,128)(2,1)} %q_ref.1) | copy-start | bytes 786436
  1.6 0.9 %copy-start.1 = (bf16[32,4096]{1,0:T(8,128)(2,1)S(1)}, bf16[32,4096]{1,0:T(8,128)(2,1)}, u32[]{:S(2)}) copy-start(bf16[32,4096]{1,0:T(8,128)(2,1)} %g_ref.1) | copy-start | bytes 786436
  2.5 0.8 %copy-start.2 = (bf16[32,512]{1,0:T(8,128)(2,1)S(1)}, bf16[32,512]{1,0:T(8,128)(2,1)}, u32[]{:S(2)}) copy-start(bf16[32,512]{1,0:T(8,128)(2,1)} %k_ref.1) | copy-start | bytes 98308
  3.3 0.8 %copy-start.3 = (bf16[32,512]{1,0:T(8,128)(2,1)S(1)}, bf16[32,512]{1,0:T(8,128)(2,1)}, u32[]{:S(2)}) copy-start(bf16[32,512]{1,0:T(8,128)(2,1)} %v_ref.1) | copy-start | bytes 98308
  4.1 0.7 %copy-start.4 = (s32[4]{0:T(128)S(1)}, s32[4]{0:T(128)}, u32[]{:S(2)}) copy-start(s32[4]{0:T(128)} %doc_ref.1) | copy-start | bytes 52

commit v2 on v1

--- a/solution.py
+++ b/solution.py
@@ -55,6 +55,7 @@
     out_recv,
     back_send,
     back_recv,
+    doc_smem,
     local_sem,
 ):
     u = lax.axis_index("ctx")
@@ -96,6 +97,8 @@
     own_copies = [
         pltpu.make_async_copy(src, dst, local_sem.at[i]) for i, (src, dst) in enumerate(own)
     ]
+    doc_copy = pltpu.make_async_copy(doc_ref, doc_smem, local_sem.at[9])
+    doc_copy.start()
     for copy in own_copies:
         copy.start()
 
@@ -149,10 +152,11 @@
             in_copy(kind, d).start()
 
     query_pos = u * block + lax.broadcasted_iota(jnp.int32, (1, block), 1)
+    doc_copy.wait()
     begins = jnp.zeros((1, block), jnp.int32)
     bound = jnp.int32(0)
-    for j in range(doc_ref.shape[0]):
-        bound = bound + doc_ref[j]
+    for j in range(doc_smem.shape[0]):
+        bound = bound + doc_smem[j]
         begins = jnp.where(query_pos >= bound, bound, begins)
     key_pos = (u - last) * block + lax.broadcasted_iota(jnp.int32, (window, block), 0)
     bias[...] = jnp.where((key_pos >= begins) & (key_pos <= query_pos), 0.0, FILL)
@@ -328,30 +332,41 @@
             out_arrival(kind, d).wait_recv()
 
 
+def place(*refs):
+    sources, targets, sem = refs[:5], refs[5:10], refs[10]
+    copies = [pltpu.make_async_copy(a, b, sem.at[i]) for i, (a, b) in enumerate(zip(sources, targets))]
+    for copy in copies:
+        copy.start()
+    for copy in copies:
+        copy.wait()
+
+
 def solution(mesh):
     ctxs, heads = mesh.shape["ctx"], mesh.shape["head"]
     reach = min(16, ctxs // 2)
 
-    def step(q, k, v, g, doc_lengths):
+    def step(*arrays):
+        q, k, v, g, doc_lengths = (pltpu.with_memory_space_constraint(a, pltpu.HBM) for a in arrays)
         tok = q.shape[0]
         block = tok * heads
         group_cols = q.shape[1] // heads
         per_group = group_cols // WIDTH
         window = reach * block
         bf16, f32 = jnp.bfloat16, jnp.float32
-        hbm = pl.BlockSpec(memory_space=pl.ANY)
+        any_space = pl.BlockSpec(memory_space=pl.ANY)
+        hbm = pl.BlockSpec(memory_space=pltpu.HBM)
         dma = pltpu.SemaphoreType.DMA
-        return pl.pallas_call(
+        results = pl.pallas_call(
             functools.partial(kernel, ctxs, heads, reach),
             out_shape=(
-                jax.ShapeDtypeStruct(q.shape, bf16),
-                jax.ShapeDtypeStruct((per_group, block), f32),
-                jax.ShapeDtypeStruct(q.shape, bf16),
-                jax.ShapeDtypeStruct(k.shape, bf16),
-                jax.ShapeDtypeStruct(k.shape, bf16),
+                pltpu.VMEM(q.shape, bf16),
+                pltpu.VMEM((per_group, block), f32),
+                pltpu.VMEM(q.shape, bf16),
+                pltpu.VMEM(k.shape, bf16),
+                pltpu.VMEM(k.shape, bf16),
             ),
-            in_specs=[hbm] * 4 + [pl.BlockSpec(memory_space=pltpu.SMEM)],
-            out_specs=(hbm,) * 5,
+            in_specs=[hbm] * 5,
+            out_specs=(any_space,) * 5,
             scratch_shapes=[
                 pltpu.VMEM((block, group_cols), bf16),
                 pltpu.VMEM((block, group_cols), bf16),
@@ -374,12 +389,21 @@
                 dma((4, heads - 1)),
                 dma((reach - 1,)),
                 dma((reach - 1,)),
-                dma((9,)),
+                pltpu.SMEM(doc_lengths.shape, jnp.int32),
+                dma((10,)),
             ],
             compiler_params=pltpu.CompilerParams(
                 collective_id=0, has_side_effects=True, vmem_limit_bytes=40 * 1024 * 1024
             ),
         )(q, k, v, g, doc_lengths)
+        return pl.pallas_call(
+            place,
+            out_shape=tuple(jax.ShapeDtypeStruct(r.shape, r.dtype) for r in results),
+            in_specs=[any_space] * 5,
+            out_specs=(hbm,) * 5,
+            scratch_shapes=[dma((5,))],
+            compiler_params=pltpu.CompilerParams(vmem_limit_bytes=40 * 1024 * 1024),
+        )(*results)
 
     placed = P(("ctx", "head"), None)
     return jax.shard_map(

time: 35.2 us -> 28.3 us (0.80)
  local copies, waits for them, and re-layouts: 7.29 us -> 0 us
  Pallas kernels: 26.9 us -> 27.5 us
    unnamed x15 -> x0, local copies, waits for them, and re-layouts: 7.29 us -> none
    pallas_call x0 -> x1, Pallas kernels: none -> 0.85 us  [step(): pl.pallas_call(place, out_shape=tuple((jax.ShapeDtypeStruct(r.shape, r.dt...]
where the time goes in v2:
time: 28.3 us; the launch traced here: 28.1 us
  Pallas kernels  27.5 us (97%)
  between operations  0.64 us (2%)
    pallas_call x1, Pallas kernels, step(): pl.pallas_call(functools.partial(kernel, ctxs, heads, reach), out_shape=(...  26.6 us
    pallas_call x1, Pallas kernels, step(): pl.pallas_call(place, out_shape=tuple((jax.ShapeDtypeStruct(r.shape, r.dt...  0.85 us

profile of v2, /device:TPU:13, one launch (start us, length us, event | category | flops | bytes accessed | tf_op | source)
XLA Modules:
  0.0 28.1 jit_solution(8749778465174067426)
XLA Ops:
  0.6 26.6 %shard_map.92 = (bf16[32,4096]{1,0:T(8,128)(2,1)S(1)}, f32[8,128]{1,0:T(8,128)S(1)}, bf16[32,4096]{1,0:T(8,128)(2,1)S(1)}, bf16[32,512]{1,0:T(8,128)(2,1)S(1)}, bf16[32,512]{1,0:T(8,128)(2,1)S(1)}) custom-call(bf16[32,4096]{1,0:T(8,128)(2,1)} %q_ref.1, bf16[32,512]{1,0:T(8,128)(2,1)} %k_ref.1, bf16[32,512]{1,0:T(8,128)(2,1)} %v_ref.1, ...), custom_call_target="tpu_custom_call" | custom-call | tf_op jit(solution)/shard_map/pallas_call | solution.py:359
  27.3 0.8 %shard_map.93 = (bf16[32,4096]{1,0:T(8,128)(2,1)}, f32[8,128]{1,0:T(8,128)}, bf16[32,4096]{1,0:T(8,128)(2,1)}, bf16[32,512]{1,0:T(8,128)(2,1)}, bf16[32,512]{1,0:T(8,128)(2,1)}) custom-call(bf16[32,4096]{1,0:T(8,128)(2,1)S(1)} %get-tuple-element.10.refs_0_, f32[8,128]{1,0:T(8,128)S(1)} %get-tuple-element.11.refs_1_, ...), custom_call_target="tpu_custom_call" | custom-call | tf_op jit(solution)/shard_map/pallas_call | solution.py:399

commit v3 on v2

--- a/solution.py
+++ b/solution.py
@@ -42,9 +42,11 @@
     dscores,
     att_buf,
     dq_buf,
-    dkv_own,
-    dkv_send,
-    dkv_recv,
+    dk_own,
+    dv_send,
+    dv_recv,
+    dk_send,
+    dk_recv,
     dkv_fin,
     norm_buf,
     in_send,
@@ -55,6 +57,7 @@
     out_recv,
     back_send,
     back_recv,
+    dv_sems,
     doc_smem,
     local_sem,
 ):
@@ -74,10 +77,19 @@
     def cols(i, width):
         return pl.ds(pl.multiple_of(i * width, width), width)
 
+    pairs = heads // 2
+    far_first = list(range(2, heads)) + [1]
+
+    def to_peer(d):
+        return lax.rem(g // 2 + d // 2, pairs) * 2 + lax.rem(lax.rem(g, 2) + d % 2, 2)
+
+    def from_peer(d):
+        return lax.rem(g // 2 + pairs - d // 2, pairs) * 2 + lax.rem(lax.rem(g, 2) + d % 2, 2)
+
     barrier = pltpu.get_barrier_semaphore()
     for d in range(1, heads):
         pl.semaphore_signal(
-            barrier, inc=1, device_id=(u, lax.rem(g + d, heads)), device_id_type=MESH
+            barrier, inc=1, device_id=(u, to_peer(d)), device_id_type=MESH
         )
     for k in range(1, reach):
         @pl.when(u + k < ctxs)
@@ -109,7 +121,8 @@
 
         @pl.when(u + k >= ctxs)
         def _():
-            dkv_recv[k - 1] = jnp.zeros((block, 2 * WIDTH), jnp.bfloat16)
+            dv_recv[k - 1] = jnp.zeros((block, WIDTH), jnp.bfloat16)
+            dk_recv[k - 1] = jnp.zeros((heads, tok, WIDTH), jnp.bfloat16)
 
     pl.semaphore_wait(
         barrier,
@@ -126,7 +139,7 @@
         return (q_buf, g_buf)[kind - 2].at[rows(i), :]
 
     def in_copy(kind, d):
-        peer = lax.rem(g + d, heads)
+        peer = to_peer(d)
         return pltpu.make_async_remote_copy(
             src_ref=in_src(kind, peer),
             dst_ref=in_dst(kind, g),
@@ -137,7 +150,7 @@
         )
 
     def in_arrival(kind, d):
-        peer = lax.rem(g + heads - d, heads)
+        peer = from_peer(d)
         return pltpu.make_async_remote_copy(
             src_ref=in_dst(kind, peer),
             dst_ref=in_dst(kind, peer),
@@ -148,8 +161,30 @@
         )
 
     for kind in range(4):
-        for d in range(1, heads):
+        for d in far_first:
             in_copy(kind, d).start()
+
+    def ctx_copy(k, d, to):
+        piece = rows(from_peer(d))
+        return pltpu.make_async_remote_copy(
+            src_ref=kv_buf.at[last, piece, :],
+            dst_ref=kv_buf.at[last - k, piece, :],
+            send_sem=ctx_send.at[k - 1, d],
+            recv_sem=ctx_recv.at[k - 1, d],
+            device_id=(to, g),
+            device_id_type=MESH,
+        )
+
+    for d in range(heads):
+        for kind in range(2):
+            if d == 0:
+                own_copies[kind].wait()
+            else:
+                in_arrival(kind, d).wait_recv()
+        for k in range(reach - 1, 0, -1):
+            @pl.when(u + k < ctxs)
+            def _():
+                ctx_copy(k, d, u + k).start()
 
     query_pos = u * block + lax.broadcasted_iota(jnp.int32, (1, block), 1)
     doc_copy.wait()
@@ -161,34 +196,14 @@
     key_pos = (u - last) * block + lax.broadcasted_iota(jnp.int32, (window, block), 0)
     bias[...] = jnp.where((key_pos >= begins) & (key_pos <= query_pos), 0.0, FILL)
 
-    own_copies[0].wait()
-    own_copies[1].wait()
-    for kind in range(2):
-        for d in range(1, heads):
-            in_arrival(kind, d).wait_recv()
-
-    def ctx_copy(k, to):
-        return pltpu.make_async_remote_copy(
-            src_ref=kv_buf.at[last],
-            dst_ref=kv_buf.at[last - k],
-            send_sem=ctx_send.at[k - 1],
-            recv_sem=ctx_recv.at[k - 1],
-            device_id=(to, g),
-            device_id_type=MESH,
-        )
-
-    for k in range(1, reach):
-        @pl.when(u + k < ctxs)
-        def _():
-            ctx_copy(k, u + k).start()
-
     own_copies[2].wait()
     for d in range(1, heads):
         in_arrival(2, d).wait_recv()
     for k in range(1, reach):
         @pl.when(u - k >= 0)
         def _():
-            ctx_copy(k, u - k).wait_recv()
+            for d in range(heads):
+                ctx_copy(k, d, u - k).wait_recv()
 
     keys = kv_buf[:, :, :WIDTH].reshape(window, WIDTH)
     values = kv_buf[:, :, WIDTH:].reshape(window, WIDTH)
@@ -208,14 +223,14 @@
     def out_src(kind, i):
         if kind < 2:
             return (att_buf, dq_buf)[kind].at[rows(i), :]
-        return dkv_fin.at[rows(i), pl.ds((kind - 2) * WIDTH, WIDTH)]
+        return dkv_fin.at[kind - 2, rows(i), :]
 
     def out_dst(kind, i):
         ref = (att_out, dq_out, dk_out, dv_out)[kind]
         return ref.at[:, cols(i, WIDTH if kind >= 2 else group_cols)]
 
     def out_copy(kind, d):
-        peer = lax.rem(g + d, heads)
+        peer = to_peer(d)
         return pltpu.make_async_remote_copy(
             src_ref=out_src(kind, peer),
             dst_ref=out_dst(kind, g),
@@ -226,7 +241,7 @@
         )
 
     def out_arrival(kind, d):
-        peer = lax.rem(g + heads - d, heads)
+        peer = from_peer(d)
         return pltpu.make_async_remote_copy(
             src_ref=out_dst(kind, peer),
             dst_ref=out_dst(kind, peer),
@@ -240,7 +255,7 @@
         return pltpu.make_async_copy(out_src(kind, g), out_dst(kind, g), local_sem.at[4 + kind])
 
     def send_out(kind):
-        for d in range(1, heads):
+        for d in far_first:
             out_copy(kind, d).start()
         own_out(kind).start()
 
@@ -251,6 +266,42 @@
     own_copies[3].wait()
     for d in range(1, heads):
         in_arrival(3, d).wait_recv()
+
+    def stacked(ref):
+        return jnp.concatenate(
+            [ref[:, h * WIDTH : (h + 1) * WIDTH] for h in range(per_group)], axis=0
+        )
+
+    def dv_copy(k, to):
+        return pltpu.make_async_remote_copy(
+            src_ref=dv_send.at[k - 1],
+            dst_ref=dv_recv.at[k - 1],
+            send_sem=dv_sems.at[0, k - 1],
+            recv_sem=dv_sems.at[1, k - 1],
+            device_id=(to, g),
+            device_id_type=MESH,
+        )
+
+    def dk_copy(k, d, to):
+        return pltpu.make_async_remote_copy(
+            src_ref=dk_send.at[k - 1, rows(to_peer(d)), :],
+            dst_ref=dk_recv.at[k - 1, d],
+            send_sem=back_send.at[k - 1, d],
+            recv_sem=back_recv.at[k - 1, d],
+            device_id=(to, g),
+            device_id_type=MESH,
+        )
+
+    def part(k):
+        return slice((last - k) * block, (last - k + 1) * block)
+
+    grads = stacked(g_buf)
+    for k in range(reach - 1, 0, -1):
+        dv_send[k - 1] = dot(probs[part(k), :], grads, NN).astype(jnp.bfloat16)
+
+        @pl.when(u - k >= 0)
+        def _():
+            dv_copy(k, u - k).start()
 
     for h in range(per_group):
         at = slice(h * WIDTH, (h + 1) * WIDTH)
@@ -261,38 +312,14 @@
             jnp.bfloat16
         )
 
-    def stacked(ref):
-        return jnp.concatenate(
-            [ref[:, h * WIDTH : (h + 1) * WIDTH] for h in range(per_group)], axis=0
-        )
-
     queries = stacked(q_buf)
-    grads = stacked(g_buf)
-
-    def back_copy(k, to):
-        return pltpu.make_async_remote_copy(
-            src_ref=dkv_send.at[k - 1],
-            dst_ref=dkv_recv.at[k - 1],
-            send_sem=back_send.at[k - 1],
-            recv_sem=back_recv.at[k - 1],
-            device_id=(to, g),
-            device_id_type=MESH,
-        )
-
-    for k in range(reach - 1, -1, -1):
-        part = slice((last - k) * block, (last - k + 1) * block)
-        dk = dot(dscores[part, :], queries, NN)
-        dv = dot(probs[part, :], grads, NN)
-        if k == 0:
-            dkv_own[:, :WIDTH] = dk
-            dkv_own[:, WIDTH:] = dv
-        else:
-            dkv_send[k - 1, :, :WIDTH] = dk.astype(jnp.bfloat16)
-            dkv_send[k - 1, :, WIDTH:] = dv.astype(jnp.bfloat16)
-
-            @pl.when(u - k >= 0)
-            def _():
-                back_copy(k, u - k).start()
+    for k in range(reach - 1, 0, -1):
+        dk_send[k - 1] = dot(dscores[part(k), :], queries, NN).astype(jnp.bfloat16)
+
+        @pl.when(u - k >= 0)
+        def _():
+            for d in far_first + [0]:
+                dk_copy(k, d, u - k).start()
 
     for h in range(per_group):
         at = slice(h * WIDTH, (h + 1) * WIDTH)
@@ -300,17 +327,32 @@
         dq_buf[:, at] = dot(ds, keys, TN).astype(jnp.bfloat16)
     send_out(1)
 
+    dv_total = dot(probs[part(0), :], grads, NN)
+    dk_own[...] = dot(dscores[part(0), :], queries, NN)
+
     for k in range(1, reach):
         @pl.when(u + k < ctxs)
         def _():
-            back_copy(k, u + k).wait_recv()
-
-    total = dkv_own[...]
-    for k in range(1, reach):
-        total = total + dkv_recv[k - 1].astype(jnp.float32)
-    dkv_fin[...] = total.astype(jnp.bfloat16)
-    send_out(2)
+            dv_copy(k, u + k).wait_recv()
+
+        dv_total = dv_total + dv_recv[k - 1].astype(jnp.float32)
+    dkv_fin[1] = dv_total.astype(jnp.bfloat16)
     send_out(3)
+
+    for d in far_first + [0]:
+        piece = rows(to_peer(d))
+        total = dk_own[piece, :]
+        for k in range(1, reach):
+            @pl.when(u + k < ctxs)
+            def _():
+                dk_copy(k, d, u + k).wait_recv()
+
+            total = total + dk_recv[k - 1, d].astype(jnp.float32)
+        dkv_fin[0, piece, :] = total.astype(jnp.bfloat16)
+        if d == 0:
+            own_out(2).start()
+        else:
+            out_copy(2, d).start()
 
     for kind in range(4):
         for d in range(1, heads):
@@ -318,11 +360,14 @@
     for k in range(1, reach):
         @pl.when(u + k < ctxs)
         def _():
-            ctx_copy(k, u + k).wait_send()
+            for d in range(heads):
+                ctx_copy(k, d, u + k).wait_send()
 
         @pl.when(u - k >= 0)
         def _():
-            back_copy(k, u - k).wait_send()
+            dv_copy(k, u - k).wait_send()
+            for d in range(heads):
+                dk_copy(k, d, u - k).wait_send()
 
     norm_copy.wait()
     for kind in range(4):
@@ -376,19 +421,22 @@
                 pltpu.VMEM((window, per_group * block), bf16),
                 pltpu.VMEM((block, group_cols), bf16),
                 pltpu.VMEM((block, group_cols), bf16),
-                pltpu.VMEM((block, 2 * WIDTH), f32),
-                pltpu.VMEM((reach - 1, block, 2 * WIDTH), bf16),
-                pltpu.VMEM((reach - 1, block, 2 * WIDTH), bf16),
-                pltpu.VMEM((block, 2 * WIDTH), bf16),
+                pltpu.VMEM((block, WIDTH), f32),
+                pltpu.VMEM((reach - 1, block, WIDTH), bf16),
+                pltpu.VMEM((reach - 1, block, WIDTH), bf16),
+                pltpu.VMEM((reach - 1, block, WIDTH), bf16),
+                pltpu.VMEM((reach - 1, heads, tok, WIDTH), bf16),
+                pltpu.VMEM((2, block, WIDTH), bf16),
                 pltpu.VMEM((per_group, block), f32),
                 dma((4, heads - 1)),
                 dma((4, heads - 1)),
-                dma((reach - 1,)),
-                dma((reach - 1,)),
+                dma((reach - 1, heads)),
+                dma((reach - 1, heads)),
                 dma((4, heads - 1)),
                 dma((4, heads - 1)),
-                dma((reach - 1,)),
-                dma((reach - 1,)),
+                dma((reach - 1, heads)),
+                dma((reach - 1, heads)),
+                dma((2, reach - 1)),
                 pltpu.SMEM(doc_lengths.shape, jnp.int32),
                 dma((10,)),
             ],

time: 28.3 us -> 25.7 us (0.908)
  Pallas kernels: 27.5 us -> 24.7 us
    pallas_call x1, Pallas kernels: 26.6 us -> 23.9 us  [step(): pl.pallas_call(functools.partial(kernel, ctxs, heads, reach), out_shape=(...]
where the time goes in v3:
time: 25.7 us; the launch traced here: 25.4 us
  Pallas kernels  24.7 us (96%)
  between operations  0.64 us (2%)
    pallas_call x1, Pallas kernels, step(): pl.pallas_call(functools.partial(kernel, ctxs, heads, reach), out_shape=(...  23.9 us
    pallas_call x1, Pallas kernels, step(): pl.pallas_call(place, out_shape=tuple((jax.ShapeDtypeStruct(r.shape, r.dt...  0.85 us

profile of v3, /device:TPU:13, one launch (start us, length us, event | category | flops | bytes accessed | tf_op | source)
XLA Modules:
  0.0 25.4 jit_solution(9983292139553719417)
XLA Ops:
  0.6 23.9 %shard_map.92 = (bf16[32,4096]{1,0:T(8,128)(2,1)S(1)}, f32[8,128]{1,0:T(8,128)S(1)}, bf16[32,4096]{1,0:T(8,128)(2,1)S(1)}, bf16[32,512]{1,0:T(8,128)(2,1)S(1)}, bf16[32,512]{1,0:T(8,128)(2,1)S(1)}) custom-call(bf16[32,4096]{1,0:T(8,128)(2,1)} %q_ref.1, bf16[32,512]{1,0:T(8,128)(2,1)} %k_ref.1, bf16[32,512]{1,0:T(8,128)(2,1)} %v_ref.1, ...), custom_call_target="tpu_custom_call" | custom-call | tf_op jit(solution)/shard_map/pallas_call | solution.py:404
  24.5 0.8 %shard_map.93 = (bf16[32,4096]{1,0:T(8,128)(2,1)}, f32[8,128]{1,0:T(8,128)}, bf16[32,4096]{1,0:T(8,128)(2,1)}, bf16[32,512]{1,0:T(8,128)(2,1)}, bf16[32,512]{1,0:T(8,128)(2,1)}) custom-call(bf16[32,4096]{1,0:T(8,128)(2,1)S(1)} %get-tuple-element.10.refs_0_, f32[8,128]{1,0:T(8,128)S(1)} %get-tuple-element.11.refs_1_, ...), custom_call_target="tpu_custom_call" | custom-call | tf_op jit(solution)/shard_map/pallas_call | solution.py:447

commit v4 on v3

--- a/solution.py
+++ b/solution.py
@@ -312,20 +312,20 @@
             jnp.bfloat16
         )
 
-    queries = stacked(q_buf)
-    for k in range(reach - 1, 0, -1):
-        dk_send[k - 1] = dot(dscores[part(k), :], queries, NN).astype(jnp.bfloat16)
-
-        @pl.when(u - k >= 0)
-        def _():
-            for d in far_first + [0]:
-                dk_copy(k, d, u - k).start()
-
     for h in range(per_group):
         at = slice(h * WIDTH, (h + 1) * WIDTH)
         ds = dscores[:, h * block : (h + 1) * block]
         dq_buf[:, at] = dot(ds, keys, TN).astype(jnp.bfloat16)
     send_out(1)
+
+    queries = stacked(q_buf)
+    for k in range(reach - 1, 0, -1):
+        dk_send[k - 1] = dot(dscores[part(k), :], queries, NN).astype(jnp.bfloat16)
+
+        @pl.when(u - k >= 0)
+        def _():
+            for d in far_first + [0]:
+                dk_copy(k, d, u - k).start()
 
     dv_total = dot(probs[part(0), :], grads, NN)
     dk_own[...] = dot(dscores[part(0), :], queries, NN)

time: 25.7 us -> 25.5 us (level)
  no operation moved by 1% of the time
where the time goes in v4:
time: 25.5 us; the launch traced here: 25.4 us
  Pallas kernels  24.7 us (97%)
  between operations  0.64 us (3%)
    pallas_call x1, Pallas kernels, step(): pl.pallas_call(functools.partial(kernel, ctxs, heads, reach), out_shape=(...  23.9 us
    pallas_call x1, Pallas kernels, step(): pl.pallas_call(place, out_shape=tuple((jax.ShapeDtypeStruct(r.shape, r.dt...  0.85 us

profile of v4, /device:TPU:13, one launch (start us, length us, event | category | flops | bytes accessed | tf_op | source)
XLA Modules:
  0.0 25.4 jit_solution(6464167145146222590)
XLA Ops:
  0.6 23.9 %shard_map.92 = (bf16[32,4096]{1,0:T(8,128)(2,1)S(1)}, f32[8,128]{1,0:T(8,128)S(1)}, bf16[32,4096]{1,0:T(8,128)(2,1)S(1)}, bf16[32,512]{1,0:T(8,128)(2,1)S(1)}, bf16[32,512]{1,0:T(8,128)(2,1)S(1)}) custom-call(bf16[32,4096]{1,0:T(8,128)(2,1)} %q_ref.1, bf16[32,512]{1,0:T(8,128)(2,1)} %k_ref.1, bf16[32,512]{1,0:T(8,128)(2,1)} %v_ref.1, ...), custom_call_target="tpu_custom_call" | custom-call | tf_op jit(solution)/shard_map/pallas_call | solution.py:404
  24.5 0.8 %shard_map.93 = (bf16[32,4096]{1,0:T(8,128)(2,1)}, f32[8,128]{1,0:T(8,128)}, bf16[32,4096]{1,0:T(8,128)(2,1)}, bf16[32,512]{1,0:T(8,128)(2,1)}, bf16[32,512]{1,0:T(8,128)(2,1)}) custom-call(bf16[32,4096]{1,0:T(8,128)(2,1)S(1)} %get-tuple-element.10.refs_0_, f32[8,128]{1,0:T(8,128)S(1)} %get-tuple-element.11.refs_1_, ...), custom_call_target="tpu_custom_call" | custom-call | tf_op jit(solution)/shard_map/pallas_call | solution.py:447
